TPU v7x, 32 devices: a whole 2x2x4 slice. The times are simulated.
32 devices in a mesh: groups: 2 (over y), rows: 4 (over z), shard: 4 (over x, core).
Axes of the slice: x: 2, y: 2, z: 4, core: 2. Of those that a mesh axis runs over, the one named last changes fastest.
Arguments:
- images: bfloat16 [8, 8, 128, 512], P(('groups', 'shard'), 'rows'), parts along dimension 0, may hold values from -6 to 6
- cotangent: bfloat16 [8, 8, 128, 512], P(('groups', 'shard'), 'rows'), parts along dimension 0, may hold values from -6 to 6
- weight_in: bfloat16 [2, 512, 512], P(None, 'shard'), may hold values from -0.25 to 0.25
- weight_group: bfloat16 [2, 144, 512], P(None, 'shard'), may hold values from -0.5 to 0.5
- weight_out: bfloat16 [2, 512, 512], P(None, 'shard'), may hold values from -0.25 to 0.25
Outputs:
- decoded: bfloat16 [8, 8, 128, 512], P(('groups', 'shard'), 'rows'), parts along dimension 0
- grad_images: bfloat16 [8, 8, 128, 512], P(('groups', 'shard'), 'rows'), parts along dimension 0
- grad_in: float32 [4, 512, 512], P('groups', 'shard'), parts along dimension 0
- grad_group: float32 [4, 144, 512], P('groups', 'shard'), parts along dimension 0
- grad_out: float32 [4, 512, 512], P('groups', 'shard'), parts along dimension 0
There are 2 independent parts, one for each index of `groups`. A program takes and returns all parts, laid end to end along the dimension named above; an argument that names none is the same for every part. Nothing has to cross between parts.
All inputs are finite; a program needn't handle non-finite values.
Results may differ from a plain program's by a relative error of at most 0.02.
Values may be sent and summed in bfloat16 or wider, within the bound.
A program may use at most 128 MiB of HBM per device.

v0:
```python
import math
import jax
import jax.numpy as jnp
from jax import lax
from jax.sharding import PartitionSpec as P

GW = 16


def extended_2(cells, sides, width):
    for axis, dim in sides:
        count = lax.axis_size(axis)
        ends = count - 1
        head = lax.slice_in_dim(cells, 0, width, axis=dim)
        tail = lax.slice_in_dim(cells, cells.shape[dim] - width, cells.shape[dim], axis=dim)
        cells = jnp.concatenate(
            [
                lax.ppermute(tail, axis, [(i, (i + 1) % count) for i in range(ends)]),
                cells,
                lax.ppermute(head, axis, [((i + 1) % count, i) for i in range(ends)]),
            ],
            axis=dim,
        )
    return cells


def silu_slope(preact):
    sigmoid_value = jax.nn.sigmoid(preact)
    return sigmoid_value * (1.0 + preact * (1.0 - sigmoid_value))


def block_kernel(full_group, hidden_width, group_width):
    sub_width = min(hidden_width, 128)
    sections = hidden_width // sub_width
    members = sub_width // group_width
    arranged = full_group.reshape(9, group_width, sections, members, group_width)
    arranged = arranged.transpose(0, 2, 3, 1, 4)
    identity = jnp.eye(members, dtype=full_group.dtype)
    expanded = arranged[:, :, :, :, None, :] * identity[None, None, :, None, :, None]
    return expanded.reshape(9, sections, sub_width, sub_width)


def grouped_taps(padded, kernel, out_rows, out_cols, flipped, pattern):
    summed = None
    for tap_index in range(9):
        row_step = tap_index // 3
        col_step = tap_index % 3
        if flipped:
            row_step = 2 - row_step
            col_step = 2 - col_step
        window = padded[:, row_step : row_step + out_rows, col_step : col_step + out_cols, :]
        window = window.reshape(-1, kernel.shape[1], kernel.shape[2])
        tap_term = jnp.einsum(
            pattern, window, kernel[tap_index], preferred_element_type=jnp.float32
        )
        summed = tap_term if summed is None else summed + tap_term
    return summed


def body(images, cotangent, weight_in, weight_group, weight_out):
    tile_count, height, across, channels = images.shape
    block_count = weight_in.shape[0]
    group_width = GW
    pixels = tile_count * height * across
    current = images.reshape(pixels, channels)
    stored = []
    for block_index in range(block_count):
        full_in, full_group, full_out = (
            lax.all_gather(weight_in[block_index], "shard", axis=0, tiled=True),
            lax.all_gather(weight_group[block_index], "shard", axis=0, tiled=True),
            lax.all_gather(weight_out[block_index], "shard", axis=0, tiled=True),
        )
        hidden_width = full_in.shape[1]
        kernel = block_kernel(full_group, hidden_width, group_width)
        pre_one = jnp.dot(current, full_in, preferred_element_type=jnp.float32)
        hidden_one = (
            jax.nn.silu(pre_one)
            .astype(jnp.bfloat16)
            .reshape(tile_count, height, across, hidden_width)
        )
        haloed = extended_2(hidden_one, (("rows", 1),), 1)
        padded_one = jnp.pad(haloed, ((0, 0), (0, 0), (1, 1), (0, 0)))
        pre_two = grouped_taps(padded_one, kernel, height, across, False, "psi,sio->pso").reshape(
            pixels, hidden_width
        )
        hidden_two = jax.nn.silu(pre_two).astype(jnp.bfloat16)
        pre_three = current.astype(jnp.float32) + jnp.dot(
            hidden_two, full_out, preferred_element_type=jnp.float32
        )
        kept_weights = None
        stored.append((current, pre_one, padded_one, pre_two, hidden_two, pre_three, kept_weights))
        current = jax.nn.silu(pre_three).astype(jnp.bfloat16)
    decoded = current.reshape(images.shape)
    grad_flow = cotangent.reshape(pixels, channels)
    shares = []
    for block_index in reversed(range(block_count)):
        flow_in, pre_one, padded_one, pre_two, hidden_two, pre_three, kept_weights = stored[
            block_index
        ]
        full_in, full_group, full_out = (
            lax.all_gather(weight_in[block_index], "shard", axis=0, tiled=True),
            lax.all_gather(weight_group[block_index], "shard", axis=0, tiled=True),
            lax.all_gather(weight_out[block_index], "shard", axis=0, tiled=True),
        )
        hidden_width = full_in.shape[1]
        kernel = block_kernel(full_group, hidden_width, group_width)
        sections = kernel.shape[1]
        sub_width = kernel.shape[2]
        members = sub_width // group_width
        slope_three = grad_flow.astype(jnp.float32) * silu_slope(pre_three)
        low_three = slope_three.astype(jnp.bfloat16)
        part_out = jnp.einsum(
            "pw,pc->wc", hidden_two, low_three, preferred_element_type=jnp.float32
        )
        slope_two = (
            jnp.einsum("pc,wc->pw", low_three, full_out, preferred_element_type=jnp.float32)
            * silu_slope(pre_two)
        ).astype(jnp.bfloat16)
        slope_sections = slope_two.reshape(pixels, sections, sub_width)
        tap_terms = []
        for tap_index in range(9):
            row_step = tap_index // 3
            col_step = tap_index % 3
            window = padded_one[:, row_step : row_step + height, col_step : col_step + across, :]
            window = window.reshape(pixels, sections, sub_width)
            blockwise = jnp.einsum(
                "psi,pso->sio", window, slope_sections, preferred_element_type=jnp.float32
            )
            blockwise = blockwise.reshape(sections, members, group_width, members, group_width)
            diagonal_part = jnp.diagonal(blockwise, axis1=1, axis2=3)
            tap_terms.append(diagonal_part.transpose(1, 0, 3, 2).reshape(group_width, hidden_width))
        part_group = jnp.stack(tap_terms).reshape(9 * group_width, hidden_width)
        slope_grid = slope_two.reshape(tile_count, height, across, hidden_width)
        padded_slope = jnp.pad(slope_grid, ((0, 0), (2, 2), (1, 1), (0, 0)))
        extended = grouped_taps(padded_slope, kernel, height + 2, across, True, "pso,sio->psi")
        extended = extended.reshape(tile_count, height + 2, across, hidden_width)
        edge_rows = jnp.concatenate([extended[:, :1], extended[:, -1:]], axis=1)
        borders = extended_2(edge_rows.astype(jnp.bfloat16), (("rows", 1),), 1).astype(
            edge_rows.dtype
        )
        back_one = extended[:, 1:-1]
        back_one = back_one.at[:, :1].add(borders[:, :1])
        back_one = back_one.at[:, -1:].add(borders[:, -1:])
        slope_one = (back_one.reshape(pixels, hidden_width) * silu_slope(pre_one)).astype(
            jnp.bfloat16
        )
        part_in = jnp.einsum("pc,pw->cw", flow_in, slope_one, preferred_element_type=jnp.float32)
        grad_flow = (
            slope_three
            + jnp.einsum("pw,cw->pc", slope_one, full_in, preferred_element_type=jnp.float32)
        ).astype(jnp.bfloat16)
        shares.append(
            (
                lax.psum_scatter(
                    part_in.astype(jnp.bfloat16), "shard", scatter_dimension=0, tiled=True
                ).astype(jnp.float32),
                lax.psum_scatter(
                    part_group.astype(jnp.bfloat16), "shard", scatter_dimension=0, tiled=True
                ).astype(jnp.float32),
                lax.psum_scatter(
                    part_out.astype(jnp.bfloat16), "shard", scatter_dimension=0, tiled=True
                ).astype(jnp.float32),
            )
        )
    shares = shares[::-1]
    totals = (
        lax.psum(jnp.stack([entry[0] for entry in shares]).astype(jnp.bfloat16), "rows").astype(
            jnp.float32
        ),
        lax.psum(jnp.stack([entry[1] for entry in shares]).astype(jnp.bfloat16), "rows").astype(
            jnp.float32
        ),
        lax.psum(jnp.stack([entry[2] for entry in shares]).astype(jnp.bfloat16), "rows").astype(
            jnp.float32
        ),
    )
    norm_factor = 1.0 / math.sqrt(pixels * lax.axis_size("rows") * lax.axis_size("shard"))
    grad_images = grad_flow.reshape(images.shape)
    return (
        decoded,
        grad_images,
        totals[0] * norm_factor,
        totals[1] * norm_factor,
        totals[2] * norm_factor,
    )


def solution(mesh):
    placed = (
        P(("groups", "shard"), "rows", None, None),
        P(("groups", "shard"), "rows", None, None),
        P(None, "shard", None),
        P(None, "shard", None),
        P(None, "shard", None),
    )
    return jax.shard_map(
        body,
        mesh=mesh,
        in_specs=placed,
        out_specs=(
            P(("groups", "shard"), "rows", None, None),
            P(("groups", "shard"), "rows", None, None),
            P("groups", "shard", None),
            P("groups", "shard", None),
            P("groups", "shard", None),
        ),
        check_vma=False,
    )
```

profile of v0, /device:TPU:0, one launch (start us, length us, event | category | flops | bytes accessed | tf_op | source)
XLA Modules:
  0.0 434.7 jit_solution(18209110213923368101)
XLA Ops:
  7.2 1.7 fusion.117
  8.9 8.6 %all-gather.1 = bf16[1,512,512]{2,1,0:T(8,128)(2,1)S(1)} all-gather(bf16[1,128,512]{2,1,0:T(8,128)(2,1)S(1)} %get-tuple-element.137), channel_id=3, replica_groups=mesh['groups'=2,'rows'=4,'shard'=4] {'shard'}, dimensions={1}, use_global_device_ids=true | all-gather | bytes 655360 | tf_op jit(solution)/shard_map/all_gather | solution.py:69
  20.6 5.2 %collective-permute-start = (bf16[1,1,128,512]{3,2,1,0:T(8,128)(2,1)}, bf16[1,1,128,512]{3,2,1,0:T(8,128)(2,1)}, u32[]{:S(2)}, u32[]{:S(2)}) collective-permute-start(bf16[1,1,128,512]{3,2,1,0:T(8,128)(2,1)} %get-tuple-element.135), channel_id=1, source_target_pairs={{0,4},{4,8},{8,12},{1,5},{5,9},{9,13},{2,6},{6,10},{10,14},{3,7},{... | collective-permute-start | bytes 393224 | tf_op jit(solution)/shard_map/ppermute | solution.py:18
  27.5 5.9 %all-gather = bf16[1,144,512]{2,0,1:T(2,128)(2,1)S(1)} all-gather(bf16[1,36,512]{2,0,1:T(2,128)(2,1)S(1)} %get-tuple-element.141), channel_id=2, replica_groups=mesh['groups'=2,'rows'=4,'shard'=4] {'shard'}, dimensions={1}, use_global_device_ids=true | all-gather | bytes 184320 | tf_op jit(solution)/shard_map/all_gather | solution.py:70
  36.6 6.0 %all-gather.3 = bf16[1,144,512]{2,0,1:T(2,128)(2,1)S(1)} all-gather(bf16[1,36,512]{2,0,1:T(2,128)(2,1)S(1)} %get-tuple-element.142), channel_id=5, replica_groups=mesh['groups'=2,'rows'=4,'shard'=4] {'shard'}, dimensions={1}, use_global_device_ids=true | all-gather | bytes 184320 | tf_op jit(solution)/shard_map/all_gather | solution.py:70
  45.9 9.3 %all-gather.4 = bf16[1,512,512]{2,1,0:T(8,128)(2,1)} all-gather(bf16[1,128,512]{2,1,0:T(8,128)(2,1)} %get-tuple-element.138), channel_id=6, replica_groups=mesh['groups'=2,'rows'=4,'shard'=4] {'shard'}, dimensions={1}, use_global_device_ids=true | all-gather | bytes 655360 | tf_op jit(solution)/shard_map/all_gather | solution.py:69
  55.2 4.4 %broadcast_multiply_fusion.1 = (bf16[9,4,8,16,8,16]{3,2,5,4,1,0:T(8,128)(2,1)S(1)}, bf16[9,4,8,16,8,16]{3,2,5,4,1,0:T(8,128)(2,1)}) fusion(bf16[8,8]{0,1:T(8,128)(2,1)S(1)} %fusion.107, bf16[9,4,8,16,16]{3,2,4,1,0:T(8,128)(2,1)S(1)} %copy.227, bf16[9,4,8,16,16]{3,2,4,1,0:T(8,128)(2,1)S(1)} %copy.238), kind=kLoop, calls=%fused_computation.19 | loop fusion | flops 1179648 | bytes 2654336 | tf_op jit(solution)/shard_map/mul | solution.py:39
  59.6 9.0 %fusion.109 = (bf16[1,4,8,16,8,16]{3,2,5,4,1,0:T(8,128)(2,1)S(1)}, bf16[1,4,8,16,8,16]{3,2,5,4,1,0:T(8,128)(2,1)S(1)}, bf16[1,4,8,16,8,16]{3,2,5,4,1,0:T(8,128)(...) fusion(bf16[9,4,8,16,8,16]{3,2,5,4,1,0:T(8,128)(2,1)} %get-tupl, ...), kind=kLoop, calls=%fused_computation.285 | loop fusion | bytes 4718592 | tf_op jit(solution)/shard_map/slice | solution.py:54
  68.6 2.0 squeeze.97
  70.6 2.6 squeeze.99
  73.2 2.6 squeeze.100
  75.9 2.6 squeeze.101
  78.5 2.6 squeeze.102
  81.1 2.6 squeeze.103
  83.7 2.6 squeeze.104
  86.3 2.6 squeeze.105
  88.9 2.6 squeeze.106
  91.5 8.8 %all-gather.2 = bf16[1,512,512]{2,1,0:T(8,128)(2,1)} all-gather(bf16[1,128,512]{2,1,0:T(8,128)(2,1)} %get-tuple-element.139), channel_id=4, replica_groups=mesh['groups'=2,'rows'=4,'shard'=4] {'shard'}, dimensions={1}, use_global_device_ids=true | all-gather | bytes 655360 | tf_op jit(solution)/shard_map/all_gather | solution.py:71
  102.6 1.7 reshape.625
  104.4 1.8 copy.294
  106.2 1.8 pad_maximum_fusion.2
  108.0 1.8 reshape.626
  109.8 1.8 copy.298
  112.4 1.8 copy.302
  114.2 1.8 reshape.628
  116.0 1.8 copy.306
  117.8 1.7 reshape.630
  119.5 1.8 copy.314
  122.1 1.8 copy.318
  123.9 1.8 reshape.632
  125.7 1.8 copy.322
  127.5 1.7 reshape.633
  129.2 1.8 copy.326
  136.6 2.1 copy.389
  138.7 1.6 convolution_add_fusion.35
  143.5 5.2 %collective-permute-start.2 = (bf16[1,1,128,512]{3,2,1,0:T(8,128)(2,1)}, bf16[1,1,128,512]{3,2,1,0:T(8,128)(2,1)}, u32[]{:S(2)}, u32[]{:S(2)}) collective-permute-start(bf16[1,1,128,512]{3,2,1,0:T(8,128)(2,1)} %get-tuple-element.131), channel_id=1, source_target_pairs={{0,4},{4,8},{8,12},{1,5},{5,9},{9,13},{2,6},{6,10},{10,14},{3,7},{... | collective-permute-start | bytes 393224 | tf_op jit(solution)/shard_map/ppermute | solution.py:18
  148.7 7.2 %all-gather.5 = bf16[1,512,512]{2,1,0:T(8,128)(2,1)} all-gather(bf16[1,128,512]{2,1,0:T(8,128)(2,1)S(1)} %copy-done.92), channel_id=7, replica_groups=mesh['groups'=2,'rows'=4,'shard'=4] {'shard'}, dimensions={1}, use_global_device_ids=true | all-gather | bytes 655360 | tf_op jit(solution)/shard_map/all_gather | solution.py:71
  155.9 2.6 squeeze.109
  158.5 2.6 squeeze.111
  161.1 2.6 squeeze.112
  163.7 2.6 squeeze.113
  166.3 2.6 squeeze.114
  168.9 2.8 squeeze.115
  186.2 2.7 convert_multiply_fusion
  198.2 1.7 pad_slice_fusion.9
  202.3 2.0 reshape.650
  204.3 2.0 reshape.651
  206.2 2.0 reshape.652
  208.2 1.9 reshape.653
  212.9 1.5 convolution_add_fusion.15
  223.7 5.2 %collective-permute-start.4 = (bf16[1,1,128,512]{3,2,1,0:T(8,128)(2,1)}, bf16[1,1,128,512]{3,2,1,0:T(8,128)(2,1)}, u32[]{:S(2)}, u32[]{:S(2)}) collective-permute-start(bf16[1,1,128,512]{3,2,1,0:T(8,128)(2,1)} %copy.401), channel_id=1, source_target_pairs={{0,4},{4,8},{8,12},{1,5},{5,9},{9,13},{2,6},{6,10},{10,14},{3,7},{... | collective-permute-start | bytes 393224 | tf_op jit(solution)/shard_map/ppermute | solution.py:18
  264.3 1.6 pad_slice_fusion
  268.3 2.0 reshape.662
  270.2 2.0 reshape.663
  272.2 2.0 reshape.664
  274.2 2.0 reshape.665
  279.0 1.5 convolution_add_fusion.7
  291.5 5.4 %collective-permute-start.6 = (bf16[1,1,128,512]{3,2,1,0:T(8,128)(2,1)}, bf16[1,1,128,512]{3,2,1,0:T(8,128)(2,1)}, u32[]{:S(2)}, u32[]{:S(2)}) collective-permute-start(bf16[1,1,128,512]{3,2,1,0:T(8,128)(2,1)} %copy.405), channel_id=1, source_target_pairs={{0,4},{4,8},{8,12},{1,5},{5,9},{9,13},{2,6},{6,10},{10,14},{3,7},{... | collective-permute-start | bytes 393224 | tf_op jit(solution)/shard_map/ppermute | solution.py:18
  308.0 2.3 convolution_convert_fusion.2
  330.3 8.6 %fusion.108 = (bf16[40,512]{1,0:T(8,128)(2,1)S(1)}, bf16[40,512]{1,0:T(8,128)(2,1)S(1)}) fusion(bf16[144,512]{1,0:T(8,128)(2,1)} %bitcast.72, bf16[144,512]{1,0:T(8,128)(2,1)S(1)} %bitcast.611), kind=kCustom, calls=%all-reduce-scatter.2 | all-reduce-scatter fusion | flops 163841 | bytes 377344
  340.3 3.7 collective-permute-start.8
  348.4 7.7 %reduce-scatter.21.cloned.1.call-done = bf16[128,512]{1,0:T(8,128)(2,1)} async-done(((bf16[512,512]{1,0:T(8,128)(2,1)}), bf16[128,512]{1,0:T(8,128)(2,1)}) %reduce-scatter.21.cloned.1.call-update) | async-done | bytes 131088
  357.9 23.0 %reduce-scatter.17.cloned.1.call-done = bf16[128,512]{1,0:T(8,128)(2,1)} async-done(((bf16[512,512]{1,0:T(8,128)(2,1)}), bf16[128,512]{1,0:T(8,128)(2,1)}) %reduce-scatter.17.cloned.1.call-update) | async-done | bytes 131088
  383.8 40.3 %all-reduce.12.cloned.1.call-done = (bf16[2,128,512]{1,2,0:T(8,128)(2,1)}, bf16[2,36,512]{2,1,0:T(8,128)(2,1)}, bf16[2,128,512]{1,2,0:T(8,128)(2,1)}) async-done(((bf16[2,128,512]{1,2,0:T(8,128)(2,1)}, bf16[2,36,512]{2,1,0:T(8,128)(2,1)}, bf16[2,128,512]{1,2,0:T(8,128)(2,1)}), (bf16[2,128,512]{1,2,0:T(8,128)(2,1)}, bf16[2,36,512]{2,1,0:T(8,128)(2,1)}, ...) | async-done | bytes 598032 | tf_op jit(solution)/shard_map/psum | solution.py:167
  (538 shorter events, 156.2 us)
Async XLA Ops:
  7.2 10.3 %copy-start.98 = (bf16[1,2,128,512]{3,2,1,0:T(8,128)(2,1)S(1)}, bf16[1,2,128,512]{3,2,1,0:T(8,128)(2,1)}, u32[]{:S(2)}) copy-start(bf16[1,2,128,512]{3,2,1,0:T(8,128)(2,1)} %param.13) | copy-start | bytes 786436
  7.2 339.2 %reduce-scatter.23.cloned.1.call-start = ((), (), s32[]{:S(2)}) async-start(), calls=%async_computation.7 | async-start | bytes 655360
  18.6 14.8 %copy-start = (bf16[256,512]{1,0:T(8,128)(2,1)}, bf16[256,512]{1,0:T(8,128)(2,1)S(1)}, u32[]{:S(2)}) copy-start(bf16[256,512]{1,0:T(8,128)(2,1)S(1)} %get-tuple-element.145) | copy-start | bytes 786436
  18.6 8.1 %copy-start.97 = (bf16[2,128,512]{2,1,0:T(8,128)(2,1)S(1)}, bf16[2,128,512]{2,1,0:T(8,128)(2,1)}, u32[]{:S(2)}) copy-start(bf16[2,128,512]{2,1,0:T(8,128)(2,1)} %param.17) | copy-start | bytes 786436
  18.6 8.8 %copy-start.93 = (bf16[2,36,512]{2,0,1:T(2,128)(2,1)S(1)}, bf16[2,36,512]{2,0,1:T(2,128)(2,1)}, u32[]{:S(2)}) copy-start(bf16[2,36,512]{2,0,1:T(2,128)(2,1)} %param.16) | copy-start | bytes 221188
  19.3 81.0 %collective-permute-start.1 = (bf16[1,1,128,512]{3,2,1,0:T(8,128)(2,1)}, bf16[1,1,128,512]{3,2,1,0:T(8,128)(2,1)}, u32[]{:S(2)}, u32[]{:S(2)}) collective-permute-start(bf16[1,1,128,512]{3,2,1,0:T(8,128)(2,1)} %get-tuple-element.136), channel_id=1, source_target_pairs={{4,0},{8,4},{12,8},{5,1},{9,5},{13,9},{6,2},{10,6},{14,10},{7,3},{... | collective-permute-start | bytes 393224 | tf_op jit(solution)/shard_map/ppermute | solution.py:20
  20.6 79.7 %collective-permute-start = (bf16[1,1,128,512]{3,2,1,0:T(8,128)(2,1)}, bf16[1,1,128,512]{3,2,1,0:T(8,128)(2,1)}, u32[]{:S(2)}, u32[]{:S(2)}) collective-permute-start(bf16[1,1,128,512]{3,2,1,0:T(8,128)(2,1)} %get-tuple-element.135), channel_id=1, source_target_pairs={{0,4},{4,8},{8,12},{1,5},{5,9},{9,13},{2,6},{6,10},{10,14},{3,7},{... | collective-permute-start | bytes 393224 | tf_op jit(solution)/shard_map/ppermute | solution.py:18
  88.9 11.5 %copy-start.1 = (bf16[256,512]{1,0:T(8,128)(2,1)S(1)}, bf16[256,512]{1,0:T(8,128)(2,1)}, u32[]{:S(2)}) copy-start(bf16[256,512]{1,0:T(8,128)(2,1)} %copy-done) | copy-start | bytes 786436
  108.0 3.6 copy-start.63
  114.2 7.1 %copy-start.62 = (bf16[1,2,128,512]{3,2,1,0:T(8,128)(2,1)S(1)}, bf16[1,2,128,512]{3,2,1,0:T(8,128)(2,1)}, u32[]{:S(2)}) copy-start(bf16[1,2,128,512]{3,2,1,0:T(8,128)(2,1)} %get-tuple-element.104) | copy-start | bytes 786436
  123.9 7.1 %copy-start.2 = (bf16[256,4,128]{0,2,1:T(8,128)(2,1)S(1)}, bf16[256,4,128]{0,2,1:T(8,128)(2,1)}, u32[]{:S(2)}) copy-start(bf16[256,4,128]{0,2,1:T(8,128)(2,1)} %copy.294) | copy-start | bytes 786436
  140.3 8.4 %copy-start.92 = (bf16[1,128,512]{2,1,0:T(8,128)(2,1)S(1)}, bf16[1,128,512]{2,1,0:T(8,128)(2,1)}, u32[]{:S(2)}) copy-start(bf16[1,128,512]{2,1,0:T(8,128)(2,1)} %get-tuple-element.140) | copy-start | bytes 393220
  142.2 33.0 %collective-permute-start.3 = (bf16[1,1,128,512]{3,2,1,0:T(8,128)(2,1)}, bf16[1,1,128,512]{3,2,1,0:T(8,128)(2,1)}, u32[]{:S(2)}, u32[]{:S(2)}) collective-permute-start(bf16[1,1,128,512]{3,2,1,0:T(8,128)(2,1)} %get-tuple-element.132), channel_id=1, source_target_pairs={{4,0},{8,4},{12,8},{5,1},{9,5},{13,9},{6,2},{10,6},{14,10},{7,3},{... | collective-permute-start | bytes 393224 | tf_op jit(solution)/shard_map/ppermute | solution.py:20
  143.5 31.8 %collective-permute-start.2 = (bf16[1,1,128,512]{3,2,1,0:T(8,128)(2,1)}, bf16[1,1,128,512]{3,2,1,0:T(8,128)(2,1)}, u32[]{:S(2)}, u32[]{:S(2)}) collective-permute-start(bf16[1,1,128,512]{3,2,1,0:T(8,128)(2,1)} %get-tuple-element.131), channel_id=1, source_target_pairs={{0,4},{4,8},{8,12},{1,5},{5,9},{9,13},{2,6},{6,10},{10,14},{3,7},{... | collective-permute-start | bytes 393224 | tf_op jit(solution)/shard_map/ppermute | solution.py:18
  173.7 10.5 %copy-start.48 = (bf16[4,128,128]{1,2,0:T(8,128)(2,1)}, bf16[4,128,128]{1,2,0:T(8,128)(2,1)S(1)}, u32[]{:S(2)}) copy-start(bf16[4,128,128]{1,2,0:T(8,128)(2,1)S(1)} %squeeze.117) | copy-start | bytes 393220
  179.1 2.2 copy-start.31
  179.4 2.1 copy-start.60
  186.2 2.8 copy-start.86
  186.2 2.8 copy-start.91
  188.9 8.2 %copy-start.119 = (f32[256,512]{1,0:T(8,128)}, f32[256,512]{1,0:T(8,128)S(1)}, u32[]{:S(2)}) copy-start(f32[256,512]{1,0:T(8,128)S(1)} %get-tuple-element.109) | copy-start | bytes 1572868
  221.0 7.8 %copy-start.76 = (bf16[4,128,128]{2,1,0:T(8,128)(2,1)S(1)}, bf16[4,128,128]{2,1,0:T(8,128)(2,1)}, u32[]{:S(2)}) copy-start(bf16[4,128,128]{2,1,0:T(8,128)(2,1)} %fusion.61) | copy-start | bytes 393220
  221.6 35.3 %collective-permute-start.5 = (bf16[1,1,128,512]{3,2,1,0:T(8,128)(2,1)S(1)}, bf16[1,1,128,512]{3,2,1,0:T(8,128)(2,1)}, u32[]{:S(2)}, u32[]{:S(2)}) collective-permute-start(bf16[1,1,128,512]{3,2,1,0:T(8,128)(2,1)S(1)} %copy.402), channel_id=1, source_target_pairs={{4,0},{8,4},{12,8},{5,1},{9,5},{13,9},{6,2},{10,6},{14,10},{7,3},{... | collective-permute-start | bytes 393224 | tf_op jit(solution)/shard_map/ppermute | solution.py:20
  223.7 33.2 %collective-permute-start.4 = (bf16[1,1,128,512]{3,2,1,0:T(8,128)(2,1)}, bf16[1,1,128,512]{3,2,1,0:T(8,128)(2,1)}, u32[]{:S(2)}, u32[]{:S(2)}) collective-permute-start(bf16[1,1,128,512]{3,2,1,0:T(8,128)(2,1)} %copy.401), channel_id=1, source_target_pairs={{0,4},{4,8},{8,12},{1,5},{5,9},{9,13},{2,6},{6,10},{10,14},{3,7},{... | collective-permute-start | bytes 393224 | tf_op jit(solution)/shard_map/ppermute | solution.py:18
  229.5 1.7 copy-start.74
  231.9 1.7 copy-start.73
  236.7 1.7 copy-start.71
  241.5 1.7 copy-start.69
  243.9 1.7 copy-start.68
  248.9 1.8 copy-start.105
  248.9 2.4 copy-start.107
  248.9 3.0 copy-start.109
  248.9 3.6 copy-start.110
  248.9 4.2 copy-start.112
  248.9 4.8 %copy-start.114 = (bf16[1,16,512]{2,1,0:T(8,128)(2,1)S(1)}, bf16[1,16,512]{2,1,0:T(8,128)(2,1)}, u32[]{:S(2)}) copy-start(bf16[1,16,512]{2,1,0:T(8,128)(2,1)} %stack_reshape.88) | copy-start | bytes 49156
  249.8 97.5 %reduce-scatter.19.cloned.1.call-start = ((), (), s32[]{:S(2)}) async-start(), calls=%async_computation.5 | async-start | bytes 655360
  256.8 2.2 copy-start.90
  260.6 2.0 copy-start.16
  261.7 1.7 copy-start.18
  287.2 9.7 %copy-start.78 = (bf16[4,128,128]{2,1,0:T(8,128)(2,1)S(1)}, bf16[4,128,128]{2,1,0:T(8,128)(2,1)}, u32[]{:S(2)}) copy-start(bf16[4,128,128]{2,1,0:T(8,128)(2,1)} %fusion.79) | copy-start | bytes 393220
  289.5 37.1 %collective-permute-start.7 = (bf16[1,1,128,512]{3,2,1,0:T(8,128)(2,1)}, bf16[1,1,128,512]{3,2,1,0:T(8,128)(2,1)}, u32[]{:S(2)}, u32[]{:S(2)}) collective-permute-start(bf16[1,1,128,512]{3,2,1,0:T(8,128)(2,1)} %copy.406), channel_id=1, source_target_pairs={{4,0},{8,4},{12,8},{5,1},{9,5},{13,9},{6,2},{10,6},{14,10},{7,3},{... | collective-permute-start | bytes 393224 | tf_op jit(solution)/shard_map/ppermute | solution.py:20
  291.5 35.1 %collective-permute-start.6 = (bf16[1,1,128,512]{3,2,1,0:T(8,128)(2,1)}, bf16[1,1,128,512]{3,2,1,0:T(8,128)(2,1)}, u32[]{:S(2)}, u32[]{:S(2)}) collective-permute-start(bf16[1,1,128,512]{3,2,1,0:T(8,128)(2,1)} %copy.405), channel_id=1, source_target_pairs={{0,4},{4,8},{8,12},{1,5},{5,9},{9,13},{2,6},{6,10},{10,14},{3,7},{... | collective-permute-start | bytes 393224 | tf_op jit(solution)/shard_map/ppermute | solution.py:18
  300.0 1.7 copy-start.75
  305.0 1.9 copy-start.5
  305.0 2.1 copy-start.13
  305.6 2.4 copy-start.95
  308.0 2.4 copy-start.113
  308.0 2.4 copy-start.115
  308.0 2.4 copy-start.7
  310.3 1.9 copy-start.11
  310.3 2.1 copy-start.65
  310.3 45.9 %reduce-scatter.21.cloned.1.call-start = ((), (), s32[]{:S(2)}) async-start(), calls=%async_computation.6 | async-start | bytes 655360
  310.4 2.0 copy-start.89
  315.2 1.7 copy-start.79
  317.6 1.7 copy-start.82
  325.9 2.7 copy-start.87
  325.9 55.0 %reduce-scatter.17.cloned.1.call-start = ((), (), s32[]{:S(2)}) async-start(), calls=%async_computation.4 | async-start | bytes 655360
  329.2 14.9 %copy-start.117 = (u32[32]{0:T(128)S(1)}, u32[32]{0:T(128)}, u32[]{:S(2)}) copy-start(u32[32]{0:T(128)} %constant.395) | copy-start | bytes 388
  330.2 93.8 %all-reduce.12.cloned.1.call-start = ((), (), s32[]{:S(2)}) async-start(), calls=%async_computation.8 | async-start | bytes 1212416 | tf_op jit(solution)/shard_map/psum | solution.py:167
  339.0 6.3 %collective-permute-start.9 = (bf16[12,512]{1,0:T(8,128)(2,1)S(1)}, bf16[12,512]{1,0:T(8,128)(2,1)S(1)}, u32[]{:S(2)}, u32[]{:S(2)}) collective-permute-start(bf16[12,512]{1,0:T(8,128)(2,1)S(1)} %slice.573), channel_id=1, source_target_pairs={{0,1},{1,2},{2,3},{4,5},{5,6},{6,7},{8,9},{9,10},{10,11},{12,13},{... | collective-permute-start | bytes 36872
  340.3 5.1 %collective-permute-start.8 = (bf16[12,512]{1,0:T(8,128)(2,1)S(1)}, bf16[12,512]{1,0:T(8,128)(2,1)S(1)}, u32[]{:S(2)}, u32[]{:S(2)}) collective-permute-start(bf16[12,512]{1,0:T(8,128)(2,1)S(1)} %slice.572), channel_id=1, source_target_pairs={{0,1},{1,2},{2,3},{4,5},{5,6},{6,7},{8,9},{9,10},{10,11},{12,13},{... | collective-permute-start | bytes 36872
  348.4 34.3 %copy-start.20 = (bf16[1,512,512]{2,1,0:T(8,128)(2,1)S(1)}, bf16[1,512,512]{2,1,0:T(8,128)(2,1)}, u32[]{:S(2)}) copy-start(bf16[1,512,512]{2,1,0:T(8,128)(2,1)} %copy-done.19) | copy-start | bytes 1572868
  348.4 34.3 %copy-start.66 = (f32[256,512]{1,0:T(8,128)S(1)}, f32[256,512]{1,0:T(8,128)}, u32[]{:S(2)}) copy-start(f32[256,512]{1,0:T(8,128)} %copy-done.64) | copy-start | bytes 1572868
  424.0 2.0 copy-start.102
  424.0 2.8 copy-start.96
  (74 other events, 86.5 us)
Sparse Core Ops, SparseCore 0:
  250.0 21.4 reduce-scatter.22
  310.4 21.4 reduce-scatter.18
  334.5 21.6 reduce-scatter.20
  359.2 21.6 reduce-scatter.16
  383.9 40.0 all-reduce.11
where the time goes:
time: 443 us; the launch traced here: 435 us
  local copies, waits for them, and re-layouts  196 us (44%)
  waiting for transfers between devices  71.1 us (16%)
  blocking collectives  54.5 us (12%)
  matrix products  44.2 us (10%)
  starting transfers between devices  31.5 us (7%)
  other arithmetic  20.9 us (5%)
  between operations  16.9 us (4%)
    reshape x52, local copies, waits for them, and re-layouts, grouped_taps(): window = window.reshape(-1, kernel.shape[1], kernel.shape[2])  52.9 us
    squeeze x18, local copies, waits for them, and re-layouts, grouped_taps(): kernel[tap_index]  42 us
    psum x1, waiting for transfers between devices, body(): lax.psum(jnp.stack([entry[0] for entry in shares]).astype(jnp.bfloat16),...  40.3 us
    unnamed x283, local copies, waits for them, and re-layouts  31.7 us
    unnamed x11, waiting for transfers between devices  30.8 us
    ppermute x4, starting transfers between devices, extended_2(): lax.ppermute(tail, axis, [(i, (i + 1) % count) for i in range(ends)])  21 us
    all_gather x2, blocking collectives, body(): lax.all_gather(weight_in[block_index], 'shard', axis=0, tiled=True)  17.9 us
    dot_general x36, matrix products, grouped_taps(): jnp.einsum(pattern, window, kernel[tap_index], preferred_element_type=jnp...  16.2 us
  transfers between devices with their start and end apart: 15, of which 3 were waited for; matrix products, arithmetic and copies ran while one was open for 38% of the time, Pallas kernels for 0%

commit v1 on v0

--- a/solution.py
+++ b/solution.py
@@ -5,6 +5,27 @@
 from jax.sharding import PartitionSpec as P
 
 GW = 16
+
+
+def collect(array, axis, dim):
+    peers, index, rows = (lax.axis_size(axis), lax.axis_index(axis), array.shape[dim])
+    right = [(i, (i + 1) % peers) for i in range(peers)]
+    backward = [(i, (i - 1) % peers) for i in range(peers)]
+    out = jnp.zeros((*array.shape[:dim], peers * rows, *array.shape[dim + 1 :]), array.dtype)
+    out = lax.dynamic_update_slice_in_dim(out, array, index * rows, axis=dim)
+    from_left = from_right = array
+    halfway = peers // 2
+    for step in range(1, halfway + 1):
+        from_left = lax.ppermute(from_left, axis, right)
+        out = lax.dynamic_update_slice_in_dim(
+            out, from_left, (index - step) % peers * rows, axis=dim
+        )
+        if step < peers - halfway:
+            from_right = lax.ppermute(from_right, axis, backward)
+            out = lax.dynamic_update_slice_in_dim(
+                out, from_right, (index + step) % peers * rows, axis=dim
+            )
+    return out
 
 
 def extended_2(cells, sides, width):
@@ -66,7 +87,7 @@
     stored = []
     for block_index in range(block_count):
         full_in, full_group, full_out = (
-            lax.all_gather(weight_in[block_index], "shard", axis=0, tiled=True),
+            collect(weight_in[block_index], "shard", 0),
             lax.all_gather(weight_group[block_index], "shard", axis=0, tiled=True),
             lax.all_gather(weight_out[block_index], "shard", axis=0, tiled=True),
         )

time: 443 us -> 488 us (1.10)
  local copies, waits for them, and re-layouts: 196 us -> 253 us
  waiting for transfers between devices: 71.1 us -> 55.7 us
    gather x18, local copies, waits for them, and re-layouts: 10.7 us -> 32.7 us  [body(): diagonal_part = jnp.diagonal(blockwise, axis1=1, axis2=3)]
    reshape x36, local copies, waits for them, and re-layouts: 15.9 us -> 34.5 us  [body(): blockwise.reshape(sections, members, group_width, members, group_width)]
    unnamed x11, waiting for transfers between devices: 30.8 us -> 21.9 us
    dynamic_update_slice x0 -> x8, local copies, waits for them, and re-layouts: none -> 8.71 us  [the longest x4 4.89 us: collect(): lax.dynamic_update_slice_in_dim(out, from_left, (index - step) % peers *...]
    another operation x20, local copies, waits for them, and re-layouts: 12.3 us -> 4.48 us  [body(): part_group = jnp.stack(tap_terms).reshape(9 * group_width, hidden_width)]
    psum x1, waiting for transfers between devices: 40.3 us -> 32.6 us  [body(): lax.psum(jnp.stack([entry[0] for entry in shares]).astype(jnp.bfloat16),...]
    unnamed x283 -> x269, local copies, waits for them, and re-layouts: 31.7 us -> 38.2 us
    reshape x52 -> x50, local copies, waits for them, and re-layouts: 52.9 us -> 57.8 us  [grouped_taps(): window = window.reshape(-1, kernel.shape[1], kernel.shape[2])]
  transfers between devices with their start and end apart: 15 -> 21, of which waited for: 3 -> 3; matrix products, arithmetic and copies ran while one was open for 38% -> 46% of each run, Pallas kernels for 0% -> 0%
where the time goes in v1:
time: 488 us; the launch traced here: 481 us
  local copies, waits for them, and re-layouts  253 us (52%)
  waiting for transfers between devices  55.7 us (11%)
  blocking collectives  53.5 us (11%)
  matrix products  42.2 us (9%)
  starting transfers between devices  36.1 us (7%)
  other arithmetic  23.6 us (5%)
  between operations  16.7 us (3%)
    reshape x50, local copies, waits for them, and re-layouts, grouped_taps(): window = window.reshape(-1, kernel.shape[1], kernel.shape[2])  57.8 us
    squeeze x18, local copies, waits for them, and re-layouts, grouped_taps(): kernel[tap_index]  44 us
    unnamed x269, local copies, waits for them, and re-layouts  38.2 us
    reshape x36, local copies, waits for them, and re-layouts, body(): blockwise.reshape(sections, members, group_width, members, group_width)  34.5 us
    gather x18, local copies, waits for them, and re-layouts, body(): diagonal_part = jnp.diagonal(blockwise, axis1=1, axis2=3)  32.7 us
    psum x1, waiting for transfers between devices, body(): lax.psum(jnp.stack([entry[0] for entry in shares]).astype(jnp.bfloat16),...  32.6 us
    unnamed x11, waiting for transfers between devices  21.9 us
    ppermute x4, starting transfers between devices, extended_2(): lax.ppermute(tail, axis, [(i, (i + 1) % count) for i in range(ends)])  20.3 us
  transfers between devices with their start and end apart: 21, of which 3 were waited for; matrix products, arithmetic and copies ran while one was open for 46% of the time, Pallas kernels for 0%

profile of v1, /device:TPU:0, one launch (start us, length us, event | category | flops | bytes accessed | tf_op | source)
XLA Modules:
  0.0 480.9 jit_solution(14241513324756811907)
XLA Ops:
  9.4 1.9 collective-permute-start.6
  14.2 7.0 %all-gather = bf16[1,144,512]{2,0,1:T(2,128)(2,1)S(1)} all-gather(bf16[1,36,512]{2,0,1:T(2,128)(2,1)S(1)} %get-tuple-element.145), channel_id=2, replica_groups=mesh['groups'=2,'rows'=4,'shard'=4] {'shard'}, dimensions={1}, use_global_device_ids=true | all-gather | bytes 184320 | tf_op jit(solution)/shard_map/all_gather | solution.py:91
  24.4 6.9 %all-gather.2 = bf16[1,144,512]{2,0,1:T(2,128)(2,1)S(1)} all-gather(bf16[1,36,512]{2,0,1:T(2,128)(2,1)S(1)} %get-tuple-element.146), channel_id=4, replica_groups=mesh['groups'=2,'rows'=4,'shard'=4] {'shard'}, dimensions={1}, use_global_device_ids=true | all-gather | bytes 184320 | tf_op jit(solution)/shard_map/all_gather | solution.py:91
  34.5 4.4 broadcast_multiply_fusion.1
  39.0 9.4 %fusion.62 = (bf16[1,4,8,16,8,16]{3,2,5,4,1,0:T(8,128)(2,1)S(1)}, bf16[1,4,8,16,8,16]{3,2,5,4,1,0:T(8,128)(2,1)S(1)}, bf16[1,4,8,16,8,16]{3,2,5,4,1,0:T(8,128)(2...) fusion(bf16[9,4,8,16,8,16]{3,2,5,4,1,0:T(8,128)(2,1)} %get-tupl, ...), kind=kLoop, calls=%fused_computation.252 | loop fusion | bytes 4718592 | tf_op jit(solution)/shard_map/slice | solution.py:75
  48.4 2.1 squeeze.97
  52.0 2.6 squeeze.99
  54.6 2.6 squeeze.100
  57.2 2.6 squeeze.101
  59.8 2.6 squeeze.102
  62.4 2.6 squeeze.103
  65.0 2.6 squeeze.104
  67.6 2.6 squeeze.105
  70.2 2.6 squeeze.106
  73.6 7.4 %all-gather.1 = bf16[1,512,512]{2,1,0:T(8,128)(2,1)S(1)} all-gather(bf16[1,128,512]{2,1,0:T(8,128)(2,1)S(1)} %get-tuple-element.136), channel_id=3, replica_groups=mesh['groups'=2,'rows'=4,'shard'=4] {'shard'}, dimensions={1}, use_global_device_ids=true | all-gather | bytes 655360 | tf_op jit(solution)/shard_map/all_gather | solution.py:92
  81.9 1.8 bitcast_convert_fusion
  83.7 9.3 %all-gather.3 = bf16[1,512,512]{2,1,0:T(8,128)(2,1)} all-gather(bf16[1,128,512]{2,1,0:T(8,128)(2,1)} %get-tuple-element.135), channel_id=5, replica_groups=mesh['groups'=2,'rows'=4,'shard'=4] {'shard'}, dimensions={1}, use_global_device_ids=true | all-gather | bytes 655360 | tf_op jit(solution)/shard_map/all_gather | solution.py:92
  99.7 2.2 multiply_convert_fusion.5
  103.4 4.6 collective-permute-start.3
  115.5 1.8 pad_maximum_fusion.2
  125.2 1.8 copy.359
  128.8 1.8 copy.366
  132.5 1.8 reshape.632
  134.3 1.8 copy.374
  149.8 5.2 %collective-permute-start.8 = (bf16[1,1,128,512]{3,2,1,0:T(8,128)(2,1)}, bf16[1,1,128,512]{3,2,1,0:T(8,128)(2,1)}, u32[]{:S(2)}, u32[]{:S(2)}) collective-permute-start(bf16[1,1,128,512]{3,2,1,0:T(8,128)(2,1)} %get-tuple-element.139), channel_id=1, source_target_pairs={{0,4},{4,8},{8,12},{1,5},{5,9},{9,13},{2,6},{6,10},{10,14},{3,7},{... | collective-permute-start | bytes 393224 | tf_op jit(solution)/shard_map/ppermute | solution.py:39
  155.0 7.2 %all-gather.4 = bf16[1,512,512]{2,1,0:T(8,128)(2,1)} all-gather(bf16[1,128,512]{2,1,0:T(8,128)(2,1)} %get-tuple-element.116), channel_id=6, replica_groups=mesh['groups'=2,'rows'=4,'shard'=4] {'shard'}, dimensions={1}, use_global_device_ids=true | all-gather | bytes 655360 | tf_op jit(solution)/shard_map/all_gather | solution.py:122
  162.2 2.6 squeeze.109
  164.8 2.6 squeeze.111
  167.4 2.6 squeeze.112
  170.0 2.6 squeeze.113
  172.6 2.6 squeeze.114
  175.2 2.6 squeeze.115
  177.8 2.8 squeeze.116
  211.7 2.0 pad_slice_fusion.9
  216.1 2.0 reshape.650
  218.0 2.0 reshape.651
  220.0 1.9 reshape.652
  222.0 2.0 reshape.653
  223.9 2.0 reshape.654
  225.9 2.0 reshape.655
  241.4 5.2 %collective-permute-start.10 = (bf16[1,1,128,512]{3,2,1,0:T(8,128)(2,1)}, bf16[1,1,128,512]{3,2,1,0:T(8,128)(2,1)}, u32[]{:S(2)}, u32[]{:S(2)}) collective-permute-start(bf16[1,1,128,512]{3,2,1,0:T(8,128)(2,1)} %copy.489), channel_id=1, source_target_pairs={{0,4},{4,8},{8,12},{1,5},{5,9},{9,13},{2,6},{6,10},{10,14},{3,7},{... | collective-permute-start | bytes 393224 | tf_op jit(solution)/shard_map/ppermute | solution.py:39
  248.5 1.8 gather_fusion.9
  253.1 1.8 gather_fusion.10
  257.0 1.8 gather_fusion.11
  261.0 1.8 gather_fusion.12
  265.0 1.8 gather_fusion.13
  269.0 1.8 gather_fusion.14
  272.9 1.8 gather_fusion.15
  302.3 2.0 reshape.662
  304.3 2.0 reshape.663
  306.3 2.0 reshape.664
  308.2 2.0 reshape.665
  310.2 2.0 reshape.666
  327.0 5.4 %collective-permute-start.12 = (bf16[1,1,128,512]{3,2,1,0:T(8,128)(2,1)}, bf16[1,1,128,512]{3,2,1,0:T(8,128)(2,1)}, u32[]{:S(2)}, u32[]{:S(2)}) collective-permute-start(bf16[1,1,128,512]{3,2,1,0:T(8,128)(2,1)} %copy.493), channel_id=1, source_target_pairs={{0,4},{4,8},{8,12},{1,5},{5,9},{9,13},{2,6},{6,10},{10,14},{3,7},{... | collective-permute-start | bytes 393224 | tf_op jit(solution)/shard_map/ppermute | solution.py:39
  346.1 1.9 gather_fusion.3
  351.7 2.1 convolution_convert_fusion.2
  362.1 1.8 gather_fusion.4
  374.0 1.8 gather_fusion.7
  378.0 1.8 gather_fusion.8
  384.6 8.9 %fusion.61 = (bf16[40,512]{1,0:T(8,128)(2,1)S(1)}, bf16[40,512]{1,0:T(8,128)(2,1)S(1)}) fusion(bf16[144,512]{1,0:T(8,128)(2,1)} %bitcast.77, bf16[144,512]{1,0:T(8,128)(2,1)S(1)} %bitcast.594), kind=kCustom, calls=%all-reduce-scatter.2 | all-reduce-scatter fusion | flops 163841 | bytes 377344
  394.9 4.3 collective-permute-start.14
  405.4 21.7 %reduce-scatter.17.cloned.1.call-done = bf16[128,512]{1,0:T(8,128)(2,1)} async-done(((bf16[512,512]{1,0:T(8,128)(2,1)}), bf16[128,512]{1,0:T(8,128)(2,1)}) %reduce-scatter.17.cloned.1.call-update) | async-done | bytes 131088
  428.9 6.8 %all-gather.5 = bf16[1,512,512]{2,1,0:T(8,128)(2,1)S(1)} all-gather(bf16[1,128,512]{2,1,0:T(8,128)(2,1)S(1)} %copy-done.100), channel_id=7, replica_groups=mesh['groups'=2,'rows'=4,'shard'=4] {'shard'}, dimensions={1}, use_global_device_ids=true | all-gather | bytes 655360 | tf_op jit(solution)/shard_map/all_gather | solution.py:122
  437.7 32.6 %all-reduce.12.cloned.1.call-done = (bf16[2,128,512]{1,2,0:T(8,128)(2,1)}, bf16[2,36,512]{2,1,0:T(8,128)(2,1)}, bf16[2,128,512]{1,2,0:T(8,128)(2,1)}) async-done(((bf16[2,128,512]{1,2,0:T(8,128)(2,1)}, bf16[2,36,512]{2,1,0:T(8,128)(2,1)}, bf16[2,128,512]{1,2,0:T(8,128)(2,1)}), (bf16[2,128,512]{1,2,0:T(8,128)(2,1)}, bf16[2,36,512]{2,1,0:T(8,128)(2,1)}, ...) | async-done | bytes 598032 | tf_op jit(solution)/shard_map/psum | solution.py:188
  (553 shorter events, 215.7 us)
Async XLA Ops:
  7.2 394.3 %reduce-scatter.23.cloned.1.call-start = ((), (), s32[]{:S(2)}) async-start(), calls=%async_computation.7 | async-start | bytes 655360
  9.0 84.1 %collective-permute-start.5 = (bf16[128,512]{1,0:T(8,128)(2,1)}, bf16[128,512]{1,0:T(8,128)(2,1)}, u32[]{:S(2)}, u32[]{:S(2)}) collective-permute-start(bf16[128,512]{1,0:T(8,128)(2,1)} %get-tuple-element.115), channel_id=1, source_target_pairs={{0,1},{1,2},{2,3},{3,0},{4,5},{5,6},{6,7},{7,4},{8,9},{9,10},{10,1... | collective-permute-start | bytes 393224 | tf_op jit(solution)/shard_map/ppermute | solution.py:19
  9.4 98.5 %collective-permute-start.6 = (bf16[128,512]{1,0:T(8,128)(2,1)}, bf16[128,512]{1,0:T(8,128)(2,1)}, u32[]{:S(2)}, u32[]{:S(2)}) collective-permute-start(bf16[128,512]{1,0:T(8,128)(2,1)} %get-tuple-element.115), channel_id=1, source_target_pairs={{0,3},{1,0},{2,1},{3,2},{4,7},{5,4},{6,5},{7,6},{8,11},{9,8},{10,9... | collective-permute-start | bytes 393224 | tf_op jit(solution)/shard_map/ppermute | solution.py:24
  11.4 82.0 %collective-permute-start = (bf16[128,512]{1,0:T(8,128)(2,1)}, bf16[128,512]{1,0:T(8,128)(2,1)}, u32[]{:S(2)}, u32[]{:S(2)}) collective-permute-start(bf16[128,512]{1,0:T(8,128)(2,1)} %get-tuple-element.114), channel_id=1, source_target_pairs={{0,1},{1,2},{2,3},{3,0},{4,5},{5,6},{6,7},{7,4},{8,9},{9,10},{10,1... | collective-permute-start | bytes 393224 | tf_op jit(solution)/shard_map/ppermute | solution.py:19
  12.0 84.2 %collective-permute-start.1 = (bf16[128,512]{1,0:T(8,128)(2,1)}, bf16[128,512]{1,0:T(8,128)(2,1)}, u32[]{:S(2)}, u32[]{:S(2)}) collective-permute-start(bf16[128,512]{1,0:T(8,128)(2,1)} %get-tuple-element.114), channel_id=1, source_target_pairs={{0,3},{1,0},{2,1},{3,2},{4,7},{5,4},{6,5},{7,6},{8,11},{9,8},{10,9... | collective-permute-start | bytes 393224 | tf_op jit(solution)/shard_map/ppermute | solution.py:24
  48.3 2.1 copy-start.65
  67.6 5.3 %copy-start.107 = (bf16[2,128,512]{2,1,0:T(8,128)(2,1)S(1)}, bf16[2,128,512]{2,1,0:T(8,128)(2,1)}, u32[]{:S(2)}) copy-start(bf16[2,128,512]{2,1,0:T(8,128)(2,1)} %param.17) | copy-start | bytes 786436
  70.2 10.8 %copy-start.70 = (bf16[1,2,128,512]{3,2,1,0:T(8,128)(2,1)S(1)}, bf16[1,2,128,512]{3,2,1,0:T(8,128)(2,1)}, u32[]{:S(2)}) copy-start(bf16[1,2,128,512]{3,2,1,0:T(8,128)(2,1)} %param.13) | copy-start | bytes 786436
  93.1 16.5 %collective-permute-start.7 = (bf16[128,512]{1,0:T(8,128)(2,1)}, bf16[128,512]{1,0:T(8,128)(2,1)}, u32[]{:S(2)}, u32[]{:S(2)}) collective-permute-start(bf16[128,512]{1,0:T(8,128)(2,1)} %collective-permute-done.5), channel_id=1, source_target_pairs={{0,1},{1,2},{2,3},{3,0},{4,5},{5,6},{6,7},{7,4},{8,9},{9,10},{10,1... | collective-permute-start | bytes 393224 | tf_op jit(solution)/shard_map/ppermute | solution.py:19
  93.4 5.7 %collective-permute-start.2 = (bf16[128,512]{1,0:T(8,128)(2,1)}, bf16[128,512]{1,0:T(8,128)(2,1)S(1)}, u32[]{:S(2)}, u32[]{:S(2)}) collective-permute-start(bf16[128,512]{1,0:T(8,128)(2,1)} %collective-permute-done), channel_id=1, source_target_pairs={{0,1},{1,2},{2,3},{3,0},{4,5},{5,6},{6,7},{7,4},{8,9},{9,10},{10,1... | collective-permute-start | bytes 393224 | tf_op jit(solution)/shard_map/ppermute | solution.py:19
  94.5 4.6 copy-start.93
  101.9 39.8 %copy-start.2 = (bf16[256,512]{0,1:T(8,128)(2,1)}, bf16[256,512]{0,1:T(8,128)(2,1)S(1)}, u32[]{:S(2)}) copy-start(bf16[256,512]{0,1:T(8,128)(2,1)S(1)} %get-tuple-element.149) | copy-start | bytes 786436
  102.1 9.0 %collective-permute-start.4 = (bf16[1,1,128,512]{3,2,1,0:T(8,128)(2,1)S(1)}, bf16[1,1,128,512]{3,2,1,0:T(8,128)(2,1)S(1)}, u32[]{:S(2)}, u32[]{:S(2)}) collective-permute-start(bf16[1,1,128,512]{3,2,1,0:T(8,128)(2,1)S(1)} %get-tuple-element.144), channel_id=1, source_target_pairs={{4,0},{8,4},{12,8},{5,1},{9,5},{13,9},{6,2},{10,6},{14,10},{7,3},{... | collective-permute-start | bytes 393224 | tf_op jit(solution)/shard_map/ppermute | solution.py:41
  103.4 7.7 %collective-permute-start.3 = (bf16[1,1,128,512]{3,2,1,0:T(8,128)(2,1)S(1)}, bf16[1,1,128,512]{3,2,1,0:T(8,128)(2,1)S(1)}, u32[]{:S(2)}, u32[]{:S(2)}) collective-permute-start(bf16[1,1,128,512]{3,2,1,0:T(8,128)(2,1)S(1)} %get-tuple-element.143), channel_id=1, source_target_pairs={{0,4},{4,8},{8,12},{1,5},{5,9},{9,13},{2,6},{6,10},{10,14},{3,7},{... | collective-permute-start | bytes 393224 | tf_op jit(solution)/shard_map/ppermute | solution.py:39
  117.4 3.6 copy-start.69
  123.5 7.1 %copy-start.68 = (bf16[1,2,128,512]{3,2,1,0:T(8,128)(2,1)S(1)}, bf16[1,2,128,512]{3,2,1,0:T(8,128)(2,1)}, u32[]{:S(2)}) copy-start(bf16[1,2,128,512]{3,2,1,0:T(8,128)(2,1)} %get-tuple-element.104) | copy-start | bytes 786436
  132.5 10.2 %copy-start.4 = (bf16[256,4,128]{0,2,1:T(8,128)(2,1)}, bf16[256,4,128]{0,2,1:T(8,128)(2,1)S(1)}, u32[]{:S(2)}) copy-start(bf16[256,4,128]{0,2,1:T(8,128)(2,1)S(1)} %copy.370) | copy-start | bytes 786436
  145.3 2.4 copy-start
  148.5 35.7 %collective-permute-start.9 = (bf16[1,1,128,512]{3,2,1,0:T(8,128)(2,1)}, bf16[1,1,128,512]{3,2,1,0:T(8,128)(2,1)}, u32[]{:S(2)}, u32[]{:S(2)}) collective-permute-start(bf16[1,1,128,512]{3,2,1,0:T(8,128)(2,1)} %get-tuple-element.140), channel_id=1, source_target_pairs={{4,0},{8,4},{12,8},{5,1},{9,5},{13,9},{6,2},{10,6},{14,10},{7,3},{... | collective-permute-start | bytes 393224 | tf_op jit(solution)/shard_map/ppermute | solution.py:41
  149.8 34.5 %collective-permute-start.8 = (bf16[1,1,128,512]{3,2,1,0:T(8,128)(2,1)}, bf16[1,1,128,512]{3,2,1,0:T(8,128)(2,1)}, u32[]{:S(2)}, u32[]{:S(2)}) collective-permute-start(bf16[1,1,128,512]{3,2,1,0:T(8,128)(2,1)} %get-tuple-element.139), channel_id=1, source_target_pairs={{0,4},{4,8},{8,12},{1,5},{5,9},{9,13},{2,6},{6,10},{10,14},{3,7},{... | collective-permute-start | bytes 393224 | tf_op jit(solution)/shard_map/ppermute | solution.py:39
  189.3 3.2 copy-start.66
  189.6 4.8 copy-start.32
  192.4 2.1 copy-start.63
  199.2 2.0 copy-start.97
  207.8 2.6 copy-start.98
  207.8 2.6 copy-start.106
  207.8 2.6 copy-start.114
  238.8 7.8 %copy-start.86 = (bf16[4,128,128]{2,1,0:T(8,128)(2,1)S(1)}, bf16[4,128,128]{2,1,0:T(8,128)(2,1)}, u32[]{:S(2)}) copy-start(bf16[4,128,128]{2,1,0:T(8,128)(2,1)} %fusion.84) | copy-start | bytes 393220
  239.3 50.6 %collective-permute-start.11 = (bf16[1,1,128,512]{3,2,1,0:T(8,128)(2,1)S(1)}, bf16[1,1,128,512]{3,2,1,0:T(8,128)(2,1)}, u32[]{:S(2)}, u32[]{:S(2)}) collective-permute-start(bf16[1,1,128,512]{3,2,1,0:T(8,128)(2,1)S(1)} %copy.490), channel_id=1, source_target_pairs={{4,0},{8,4},{12,8},{5,1},{9,5},{13,9},{6,2},{10,6},{14,10},{7,3},{... | collective-permute-start | bytes 393224 | tf_op jit(solution)/shard_map/ppermute | solution.py:41
  241.4 48.5 %collective-permute-start.10 = (bf16[1,1,128,512]{3,2,1,0:T(8,128)(2,1)}, bf16[1,1,128,512]{3,2,1,0:T(8,128)(2,1)}, u32[]{:S(2)}, u32[]{:S(2)}) collective-permute-start(bf16[1,1,128,512]{3,2,1,0:T(8,128)(2,1)} %copy.489), channel_id=1, source_target_pairs={{0,4},{4,8},{8,12},{1,5},{5,9},{9,13},{2,6},{6,10},{10,14},{3,7},{... | collective-permute-start | bytes 393224 | tf_op jit(solution)/shard_map/ppermute | solution.py:39
  247.3 3.9 copy-start.84
  251.9 3.3 copy-start.83
  255.8 3.3 copy-start.82
  259.8 3.3 copy-start.81
  263.8 3.3 copy-start.80
  267.7 3.3 copy-start.79
  271.7 3.3 copy-start.78
  275.7 3.3 copy-start.77
  283.0 119.5 %reduce-scatter.19.cloned.1.call-start = ((), (), s32[]{:S(2)}) async-start(), calls=%async_computation.5 | async-start | bytes 655360
  322.7 9.7 %copy-start.88 = (bf16[4,128,128]{2,1,0:T(8,128)(2,1)S(1)}, bf16[4,128,128]{2,1,0:T(8,128)(2,1)}, u32[]{:S(2)}) copy-start(bf16[4,128,128]{2,1,0:T(8,128)(2,1)} %fusion.75) | copy-start | bytes 393220
  324.9 55.3 %collective-permute-start.13 = (bf16[1,1,128,512]{3,2,1,0:T(8,128)(2,1)}, bf16[1,1,128,512]{3,2,1,0:T(8,128)(2,1)}, u32[]{:S(2)}, u32[]{:S(2)}) collective-permute-start(bf16[1,1,128,512]{3,2,1,0:T(8,128)(2,1)} %copy.494), channel_id=1, source_target_pairs={{4,0},{8,4},{12,8},{5,1},{9,5},{13,9},{6,2},{10,6},{14,10},{7,3},{... | collective-permute-start | bytes 393224 | tf_op jit(solution)/shard_map/ppermute | solution.py:41
  327.0 53.3 %collective-permute-start.12 = (bf16[1,1,128,512]{3,2,1,0:T(8,128)(2,1)}, bf16[1,1,128,512]{3,2,1,0:T(8,128)(2,1)}, u32[]{:S(2)}, u32[]{:S(2)}) collective-permute-start(bf16[1,1,128,512]{3,2,1,0:T(8,128)(2,1)} %copy.493), channel_id=1, source_target_pairs={{0,4},{4,8},{8,12},{1,5},{5,9},{9,13},{2,6},{6,10},{10,14},{3,7},{... | collective-permute-start | bytes 393224 | tf_op jit(solution)/shard_map/ppermute | solution.py:39
  333.0 3.3 copy-start.87
  337.0 3.3 copy-start.85
  341.0 3.3 copy-start.89
  346.1 4.4 copy-start.3
  346.1 5.3 %copy-start.11 = (bf16[256,4,128]{0,2,1:T(8,128)(2,1)S(1)}, bf16[256,4,128]{0,2,1:T(8,128)(2,1)}, u32[]{:S(2)}) copy-start(bf16[256,4,128]{0,2,1:T(8,128)(2,1)} %copy.366) | copy-start | bytes 786436
  348.1 3.5 copy-start.76
  351.6 3.4 copy-start.5
  353.8 2.2 copy-start.7
  353.8 2.4 copy-start.9
  353.8 2.7 copy-start.1
  353.8 49.8 %reduce-scatter.21.cloned.1.call-start = ((), (), s32[]{:S(2)}) async-start(), calls=%async_computation.6 | async-start | bytes 655360
  364.9 3.3 copy-start.90
  378.0 2.2 copy-start.109
  380.1 47.0 %reduce-scatter.17.cloned.1.call-start = ((), (), s32[]{:S(2)}) async-start(), calls=%async_computation.4 | async-start | bytes 655360
  383.5 15.7 %copy-start.112 = (u32[32]{0:T(128)S(1)}, u32[32]{0:T(128)}, u32[]{:S(2)}) copy-start(u32[32]{0:T(128)} %constant.436) | copy-start | bytes 388
  384.5 85.8 %all-reduce.12.cloned.1.call-start = ((), (), s32[]{:S(2)}) async-start(), calls=%async_computation.8 | async-start | bytes 1212416 | tf_op jit(solution)/shard_map/psum | solution.py:188
  393.5 6.9 %collective-permute-start.15 = (bf16[12,512]{1,0:T(8,128)(2,1)S(1)}, bf16[12,512]{1,0:T(8,128)(2,1)S(1)}, u32[]{:S(2)}, u32[]{:S(2)}) collective-permute-start(bf16[12,512]{1,0:T(8,128)(2,1)S(1)} %slice.573), channel_id=1, source_target_pairs={{0,1},{1,2},{2,3},{4,5},{5,6},{6,7},{8,9},{9,10},{10,11},{12,13},{... | collective-permute-start | bytes 36872
  394.9 5.7 %collective-permute-start.14 = (bf16[12,512]{1,0:T(8,128)(2,1)S(1)}, bf16[12,512]{1,0:T(8,128)(2,1)S(1)}, u32[]{:S(2)}, u32[]{:S(2)}) collective-permute-start(bf16[12,512]{1,0:T(8,128)(2,1)S(1)} %slice.572), channel_id=1, source_target_pairs={{0,1},{1,2},{2,3},{4,5},{5,6},{6,7},{8,9},{9,10},{10,11},{12,13},{... | collective-permute-start | bytes 36872
  403.6 25.4 %copy-start.100 = (bf16[1,128,512]{2,1,0:T(8,128)(2,1)S(1)}, bf16[1,128,512]{2,1,0:T(8,128)(2,1)}, u32[]{:S(2)}) copy-start(bf16[1,128,512]{2,1,0:T(8,128)(2,1)} %get-tuple-element.113) | copy-start | bytes 393220
  405.4 30.3 %copy-start.108 = (bf16[256,512]{0,1:T(8,128)(2,1)S(1)}, bf16[256,512]{0,1:T(8,128)(2,1)}, u32[]{:S(2)}) copy-start(bf16[256,512]{0,1:T(8,128)(2,1)} %get-tuple-element.153) | copy-start | bytes 786436
  470.3 2.0 copy-start.110
  470.3 2.8 copy-start.104
  (72 other events, 82.5 us)
Sparse Core Ops, SparseCore 0:
  283.1 21.9 reduce-scatter.22
  353.9 21.9 reduce-scatter.18
  380.3 21.9 reduce-scatter.20
  405.3 21.7 reduce-scatter.16
  430.1 40.1 all-reduce.11
